TPU v7x, 512 devices: a whole 4x8x8 slice. The times are simulated.
512 devices in a mesh: rep: 64 (over x, z_lo, y), fsdp: 8 (over z_hi, core).
Axes of the slice: x: 4, y: 8, z: 8 (z_hi: 4, z_lo: 2; z = z_hi * 2 + z_lo), core: 2. Of those that a mesh axis runs over, the one named last changes fastest.
Arguments:
- weights: bfloat16 [64, 2048, 2048], P('rep', None, 'fsdp'), may hold values from -0.125 to 0.125
- head_out: bfloat16 [64, 1024, 2048], P('rep', 'fsdp'), may hold values from -6 to 6
- token_ids: int32 [64, 1024], P('rep', 'fsdp'), may hold values from 0 to 31999, as said below
- embed_table: bfloat16 [32000, 2048], P('rep', 'fsdp'), may hold values from -6 to 6
- norm_gain: float32 [2048], replicated, may hold values from 0.1 to 1.9
- cotangent: bfloat16 [64, 1024, 2048], P('rep', 'fsdp'), may hold values from -6 to 6
- mix_step: int32 [1], replicated, may hold values from 0 to 999
Outputs:
- new_weights: bfloat16 [64, 2048, 2048], P('rep', None, 'fsdp')
Inputs may be any that keep to these rules, and one draw needn't show every extreme that they name: `token_ids`: in each replica's 1024 tokens at most 32 ids lie in any one block of 500 ids that starts at a multiple of 500, and in each replica some block holds exactly 32 of them.
All inputs are finite; a program needn't handle non-finite values.
Results may differ from a plain program's by a relative error of at most 0.0039.
Values may be sent and summed in bfloat16 or wider, within the bound.
A program may use at most 64 MiB of HBM per device.

v0:
```python
import jax
import jax.numpy as jnp
from jax import lax
from jax.sharding import PartitionSpec as P

MIXBITS = 4


EPS = 1e-05
RATE = 0.5


def for_sending(shard):
    return jax.tree.map(lambda a: a.astype(jnp.bfloat16) if a.dtype == jnp.float32 else a, shard)


def partner(block, axis, apart):
    count = lax.axis_size(axis)
    route = []
    for low in range(count):
        high = low | 1 << apart
        if high != low and high < count:
            route += [(low, high), (high, low)]
    return lax.ppermute(block, axis, route)


def partner_copy(shard_in, mix_step):
    mix_level = mix_step[0] % MIXBITS

    def make_branch(level_bit):

        def branch(values):
            return jax.tree.map(
                lambda part, own: part.astype(own.dtype),
                partner(for_sending(values), "rep", level_bit),
                values,
            )

        return branch

    return lax.switch(mix_level, [make_branch(level_bit) for level_bit in range(MIXBITS)], shard_in)


def embed_columns(token_ids, embed_table):
    replica_ids = lax.all_gather(token_ids, "fsdp", axis=1, tiled=True)[0]
    groups = lax.axis_size("rep")
    rows_each = embed_table.shape[0]
    replica_rows = replica_ids.shape[0]
    capacity = max(2, 2 * replica_rows // groups)
    owners = replica_ids // rows_each
    onehot = (owners[:, None] == jnp.arange(groups, dtype=jnp.int32)[None, :]).astype(jnp.int32)
    slot_rank = jnp.sum((jnp.cumsum(onehot, axis=0) - 1) * onehot, axis=1)
    position = owners * capacity + slot_rank
    local_row = replica_ids - owners * rows_each
    requests = jnp.full((groups * capacity,), -1, jnp.int32).at[position].set(local_row)
    requests = requests.reshape(groups, capacity)
    requested = lax.all_to_all(requests, "rep", split_axis=0, concat_axis=0, tiled=True)
    valid_slot = requested >= 0
    picked = jnp.take(embed_table, jnp.clip(requested, 0, rows_each - 1), axis=0)
    picked = jnp.where(valid_slot[..., None], picked, jnp.zeros((), embed_table.dtype))
    fetched = lax.all_to_all(picked, "rep", split_axis=0, concat_axis=0, tiled=True)
    return fetched.reshape(groups * capacity, embed_table.shape[1])[position]


def local(weights, head_out, token_ids, embed_table, norm_gain, cotangent, mix_step):
    partner_shard = partner_copy(weights, mix_step)
    mixed = (weights[0].astype(jnp.float32) + partner_shard[0].astype(jnp.float32)) * 0.5
    mixed_weights = mixed.astype(jnp.bfloat16)
    head_rows = head_out[0]
    embed_cols = embed_columns(token_ids, embed_table)
    replica_rows = head_rows.shape[0] * lax.axis_size("fsdp")
    projected = jnp.dot(
        head_rows,
        lax.all_gather(mixed_weights, "fsdp", axis=1, tiled=True),
        preferred_element_type=jnp.float32,
    )
    embed_own = lax.all_to_all(embed_cols, "fsdp", split_axis=0, concat_axis=1, tiled=True)
    stream = embed_own.astype(jnp.float32) + projected
    inverse = 1.0 / jnp.sqrt(jnp.mean(stream * stream, axis=-1, keepdims=True) + EPS)
    weighted = norm_gain * cotangent[0].astype(jnp.float32)
    drift = jnp.mean(weighted * stream, axis=-1, keepdims=True)
    stream_grad = (weighted * inverse - stream * drift * inverse * inverse * inverse).astype(
        jnp.bfloat16
    )
    grad_cols = lax.all_to_all(stream_grad, "fsdp", split_axis=1, concat_axis=0, tiled=True)
    initial = jnp.zeros(mixed.shape, jnp.float32)
    part_rows = lax.all_gather(head_rows, "fsdp", axis=0, tiled=True)
    grad_rows = lax.slice_in_dim(grad_cols, 0, part_rows.shape[0], axis=0)
    weight_grad = initial + lax.dot_general(
        part_rows, grad_rows, (((0,), (0,)), ((), ())), preferred_element_type=jnp.float32
    )
    weight_grad = weight_grad / replica_rows
    return (mixed - RATE * weight_grad).astype(jnp.bfloat16)[None]


def solution(mesh):
    return jax.shard_map(
        local,
        mesh=mesh,
        in_specs=(
            P("rep", None, "fsdp"),
            P("rep", "fsdp", None),
            P("rep", "fsdp"),
            P("rep", "fsdp"),
            P(),
            P("rep", "fsdp", None),
            P(),
        ),
        out_specs=P("rep", None, "fsdp"),
        check_vma=False,
    )
```

profile of v0, /device:TPU:1, one launch (start us, length us, event | category | flops | bytes accessed | tf_op | source)
XLA Modules:
  0.0 245.6 jit_solution(13891876235571914343)
XLA Ops:
  6.5 0.0 copy-start
  6.5 0.0 all-gather.4.cloned.1.call-start
  7.3 1.5 copy.30
  8.7 22.3 %conditional.4 = (bf16[2048,256]{1,0:T(8,128)(2,1)}) conditional(s32[]{:T(128)} %clamp.15, bf16[1,2048,256]{2,1,0:T(8,128)(2,1)} %param.11, bf16[1,2048,256]{2,1,0:T(8,128)(2,1)} %param.11, bf16[1,2048,256]{2,1,0:T(8,128)(2,1)} %param.11, bf16[1,2048,256]{2,1,0:T(8,128)(2,1)} %param.11), branch_computations={%region_0.1_spmd, %region_1.2_spmd, %region_2.3_spmd, %region_3.4_... | conditional | bytes 4194352
  8.8 4.0 %collective-permute-start = (bf16[1,2048,256]{2,1,0:T(8,128)(2,1)}, bf16[1,2048,256]{2,1,0:T(8,128)(2,1)}, u32[]{:S(2)}, u32[]{:S(2)}) collective-permute-start(bf16[1,2048,256]{2,1,0:T(8,128)(2,1)} %param), channel_id=1, source_target_pairs={{0,8},{8,0},{16,24},{24,16},{32,40},{40,32},{48,56},{56,48},{64,72... | collective-permute-start | bytes 3145736 | tf_op jit(solution)/shard_map/cond/branch_0_fun/ppermute | solution.py:24
  12.8 18.3 %collective-permute-done = bf16[1,2048,256]{2,1,0:T(8,128)(2,1)} collective-permute-done((bf16[1,2048,256]{2,1,0:T(8,128)(2,1)}, bf16[1,2048,256]{2,1,0:T(8,128)(2,1)}, u32[]{:S(2)}, u32[]{:S(2)}) %collective-permute-start) | collective-permute-done | bytes 1048608 | tf_op jit(solution)/shard_map/cond/branch_0_fun/ppermute | solution.py:24
  31.1 1.5 copy.31
  32.6 0.0 copy-start.3
  32.6 1.4 fusion.19
  34.0 0.0 all-gather.4.cloned.1.call-update
  34.0 0.0 all-gather.6.cloned.1.call-start
  34.1 0.7 all-gather.6.cloned.1.call-update
  34.8 0.0 copy-done.3
  34.8 23.8 %all_gather.9 = s32[1,1024]{1,0:T(1,128)S(1)} all-gather(s32[1,128]{1,0:T(1,128)S(1)} %copy-done.3), channel_id=1, replica_groups=mesh['rep'=64,'fsdp'=8] {'fsdp'}, dimensions={1}, use_global_device_ids=true | all-gather | bytes 4608 | tf_op jit(solution)/shard_map/all_gather | solution.py:45
  58.7 18.0 %reduce-window.6 = s32[64,8,128]{2,1,0:T(8,128)S(1)} reduce-window(s32[64,8,128]{2,1,0:T(8,128)S(1)} %fusion.28, s32[]{:T(128)} %constant.30.clone.1), window={size=1x1x128 pad=0_0x0_0x127_0}, to_apply=%region_4.5 | reduce-window | flops 8323072 | bytes 524292 | tf_op jit(solution)/shard_map/reduce-window
  76.7 0.1 slice.12
  76.8 0.1 copy.33
  77.0 0.1 copy.34
  77.1 0.1 add_add_fusion
  77.3 0.1 fusion.27
  77.4 4.3 %scatter_custom_fusion = s32[2048]{0:T(1024)S(1)} fusion(s32[1024]{0:T(1024)S(1)} %bitcast.114, s32[1024]{0:T(1024)S(1)} %get-tuple-element.22, s32[]{:T(128)} %constant.34.clone.1), kind=kCustom, calls=%fused_computation.46 | custom fusion | bytes 8196 | tf_op jit(solution)/shard_map/scatter | solution.py:55
  81.7 0.1 all_to_all.33
  81.8 36.5 %all_to_all.46 = s32[64,1,32]{2,1,0:T(1,128)S(1)} all-to-all(s32[64,1,32]{2,1,0:T(1,128)S(1)} %bitcast.110), channel_id=1, replica_groups=mesh['rep'=64,'fsdp'=8] {'rep'}, dimensions={0} | all-to-all | bytes 16384 | tf_op jit(solution)/shard_map/all_to_all | solution.py:57
  118.2 0.1 copy.36
  118.3 0.1 copy.40
  118.4 0.1 reshape.188
  118.5 0.1 copy.37
  118.6 0.1 copy.39
  118.7 0.0 copy-done
  118.7 7.5 %gather_fusion = bf16[2048,256]{1,0:T(8,128)(2,1)S(1)} fusion(bf16[500,256]{1,0:T(8,128)(2,1)S(1)} %copy-done, s32[2048]{0:T(1024)S(1)} %broadcast_clamp_fusion), kind=kCustom, calls=%fused_computation | custom fusion | bytes 2105344 | tf_op jit(solution)/shard_map/jit(_take)/gather | solution.py:59
  126.3 1.5 select_select_fusion
  127.8 8.6 %all-to-all-start.1 = ((bf16[64,32,256]{2,1,0:T(8,128)(2,1)}), bf16[64,32,256]{2,1,0:T(8,128)(2,1)S(1)}, u32[]{:S(2)}, u32[]{:S(2)}) async-start(bf16[64,32,256]{2,1,0:T(8,128)(2,1)} %select_select_fusion), calls=%async_computation.1 | async-start | bytes 2097152 | tf_op jit(solution)/shard_map/all_to_all | solution.py:61
  136.4 27.0 %all-to-all-done.1 = bf16[64,32,256]{2,1,0:T(8,128)(2,1)S(1)} async-done(((bf16[64,32,256]{2,1,0:T(8,128)(2,1)}), bf16[64,32,256]{2,1,0:T(8,128)(2,1)S(1)}, u32[]{:S(2)}, u32[]{:S(2)}) %all-to-all-start.1) | async-done | bytes 1048608 | tf_op jit(solution)/shard_map/all_to_all | solution.py:61
  163.4 5.0 %gather_fusion.1 = bf16[1024,256]{1,0:T(8,128)(2,1)} fusion(bf16[2048,256]{1,0:T(8,128)(2,1)S(1)} %bitcast.103, s32[1024]{0:T(1024)S(1)} %broadcast_clamp_fusion.1), kind=kCustom, calls=%fused_computation.1 | custom fusion | bytes 1052672 | tf_op jit(solution)/shard_map/gather | solution.py:62
  168.3 2.0 copy.41
  170.4 6.6 %all-to-all-start.2 = ((bf16[8,128,256]{1,2,0:T(8,128)(2,1)}), bf16[8,128,256]{1,2,0:T(8,128)(2,1)S(1)}, u32[]{:S(2)}, u32[]{:S(2)}) async-start(bf16[8,128,256]{1,2,0:T(8,128)(2,1)} %copy.41), calls=%async_computation.2 | async-start | bytes 1048576 | tf_op jit(solution)/shard_map/all_to_all | solution.py:77
  177.0 1.3 copy.32
  178.3 24.1 %all-to-all-done.2 = bf16[8,128,256]{1,2,0:T(8,128)(2,1)S(1)} async-done(((bf16[8,128,256]{1,2,0:T(8,128)(2,1)}), bf16[8,128,256]{1,2,0:T(8,128)(2,1)S(1)}, u32[]{:S(2)}, u32[]{:S(2)}) %all-to-all-start.2) | async-done | bytes 524320 | tf_op jit(solution)/shard_map/all_to_all | solution.py:77
  202.4 1.0 convert_element_type.63
  203.4 0.0 copy-done.2
  203.4 6.2 %multiply_reduce_fusion = (f32[128]{0:T(128)S(1)}, f32[128]{0:T(128)S(1)}, f32[128,2048]{0,1:T(8,128)S(1)}) fusion(bf16[1,128,2048]{1,2,0:T(8,128)(2,1)S(1)} %copy.32, f32[2048]{0:T(1024)S(1)} %copy-done.2, f32[128,2048]{0,1:T(8,128)} %bitcast.108, bf16[2048,2048]{0,1:T(8,128)(2,1)} %all-gather.4.cloned.1.call-done, bf16[1,128,2048]{2,1,0:T(8,128)(2,1)} %param.12), kind=kOutput, calls=%fused_computation.21 | convolution fusion | flops 1075576576 | bytes 11543552 | tf_op jit(solution)/shard_map/dot_general | solution.py:72
  209.6 0.4 fusion.23
  210.1 1.0 copy.42
  211.1 7.3 %all-to-all-start.3 = ((bf16[128,8,256]{2,0,1:T(8,128)(2,1)}), bf16[128,8,256]{2,0,1:T(8,128)(2,1)S(1)}, u32[]{:S(2)}, u32[]{:S(2)}) async-start(bf16[128,8,256]{2,0,1:T(8,128)(2,1)} %copy.42), calls=%async_computation.3 | async-start | bytes 1048576 | tf_op jit(solution)/shard_map/all_to_all | solution.py:85
  218.4 14.5 %all-to-all-done.3 = bf16[128,8,256]{2,0,1:T(8,128)(2,1)S(1)} async-done(((bf16[128,8,256]{2,0,1:T(8,128)(2,1)}), bf16[128,8,256]{2,0,1:T(8,128)(2,1)S(1)}, u32[]{:S(2)}, u32[]{:S(2)}) %all-to-all-start.3) | async-done | bytes 524320 | tf_op jit(solution)/shard_map/all_to_all | solution.py:85
  232.9 0.8 copy-done.1
  233.7 3.8 %fusion.14 = bf16[1,2048,256]{1,2,0:T(8,128)(2,1)S(1)} fusion(bf16[1024,256]{1,0:T(8,128)(2,1)} %bitcast.105, bf16[1,1024,2048]{2,1,0:T(8,128)(2,1)} %all-gather.6.cloned.1.call-done, bf16[2048,256]{0,1:T(8,128)(2,1)S(1)} %copy.31, bf16[1,2048,256]{1,2,0:T(8,128)(2,1)S(1)} %copy.30), kind=kOutput, calls=%fused_computation.9 | convolution fusion | flops 1077411840 | bytes 7864320 | tf_op jit(solution)/shard_map/dot_general | solution.py:89
  237.5 1.3 copy.43
  (18 shorter events, 0.2 us)
Async XLA Ops:
  6.5 112.2 %copy-start = (bf16[500,256]{1,0:T(8,128)(2,1)S(1)}, bf16[500,256]{1,0:T(8,128)(2,1)}, u32[]{:S(2)}) copy-start(bf16[500,256]{1,0:T(8,128)(2,1)} %param.14) | copy-start | bytes 768004
  6.5 196.9 %all-gather.4.cloned.1.call-start = ((), (), s32[]{:S(2)}) async-start(), calls=%async_computation.4 | async-start | bytes 9437184 | tf_op jit(solution)/shard_map/all_gather | solution.py:74
  8.8 22.3 %collective-permute-start = (bf16[1,2048,256]{2,1,0:T(8,128)(2,1)}, bf16[1,2048,256]{2,1,0:T(8,128)(2,1)}, u32[]{:S(2)}, u32[]{:S(2)}) collective-permute-start(bf16[1,2048,256]{2,1,0:T(8,128)(2,1)} %param), channel_id=1, source_target_pairs={{0,8},{8,0},{16,24},{24,16},{32,40},{40,32},{48,56},{56,48},{64,72... | collective-permute-start | bytes 3145736 | tf_op jit(solution)/shard_map/cond/branch_0_fun/ppermute | solution.py:24
  32.6 2.2 copy-start.3
  34.0 184.4 %all-gather.6.cloned.1.call-start = ((), (), s32[]{:S(2)}) async-start(), calls=%async_computation.5 | async-start | bytes 4718592 | tf_op jit(solution)/shard_map/all_gather | solution.py:87
  127.8 35.6 %all-to-all-start.1 = ((bf16[64,32,256]{2,1,0:T(8,128)(2,1)}), bf16[64,32,256]{2,1,0:T(8,128)(2,1)S(1)}, u32[]{:S(2)}, u32[]{:S(2)}) async-start(bf16[64,32,256]{2,1,0:T(8,128)(2,1)} %select_select_fusion), calls=%async_computation.1 | async-start | bytes 2097152 | tf_op jit(solution)/shard_map/all_to_all | solution.py:61
  170.4 33.1 %copy-start.2 = (f32[2048]{0:T(1024)S(1)}, f32[2048]{0:T(1024)}, u32[]{:S(2)}) copy-start(f32[2048]{0:T(1024)} %param.15) | copy-start | bytes 24580
  170.4 32.0 %all-to-all-start.2 = ((bf16[8,128,256]{1,2,0:T(8,128)(2,1)}), bf16[8,128,256]{1,2,0:T(8,128)(2,1)S(1)}, u32[]{:S(2)}, u32[]{:S(2)}) async-start(bf16[8,128,256]{1,2,0:T(8,128)(2,1)} %copy.41), calls=%async_computation.2 | async-start | bytes 1048576 | tf_op jit(solution)/shard_map/all_to_all | solution.py:77
  211.1 21.8 %all-to-all-start.3 = ((bf16[128,8,256]{2,0,1:T(8,128)(2,1)}), bf16[128,8,256]{2,0,1:T(8,128)(2,1)S(1)}, u32[]{:S(2)}, u32[]{:S(2)}) async-start(bf16[128,8,256]{2,0,1:T(8,128)(2,1)} %copy.42), calls=%async_computation.3 | async-start | bytes 1048576 | tf_op jit(solution)/shard_map/all_to_all | solution.py:85
  232.9 0.8 copy-start.1
Sparse Core Ops, SparseCore 0:
  34.2 101.8 all-gather.3
  138.2 70.1 all-gather.5
where the time goes:
time: 247 us; the launch traced here: 246 us
  waiting for transfers between devices  84.5 us (34%)
  blocking collectives  60.3 us (24%)
  local copies, waits for them, and re-layouts  27.1 us (11%)
  starting transfers between devices  26.6 us (11%)
  other arithmetic  22.8 us (9%)
  between operations  14.3 us (6%)
  matrix products  9.98 us (4%)
    all_to_all x1, blocking collectives, embed_columns(): lax.all_to_all(requests, 'rep', split_axis=0, concat_axis=0, tiled=True)  36.5 us
    all_to_all x1, waiting for transfers between devices, embed_columns(): lax.all_to_all(picked, 'rep', split_axis=0, concat_axis=0, tiled=True)  27 us
    all_to_all x1, waiting for transfers between devices, local(): lax.all_to_all(embed_cols, 'fsdp', split_axis=0, concat_axis=1, tiled=True)  24.1 us
    all_gather x1, blocking collectives, embed_columns(): replica_ids = lax.all_gather(token_ids, 'fsdp', axis=1, tiled=True)[0]  23.8 us
    ppermute x1, waiting for transfers between devices, partner(): return lax.ppermute(block, axis, route)  18.3 us
    another operation x2, other arithmetic  18 us
    all_to_all x1, waiting for transfers between devices, local(): lax.all_to_all(stream_grad, 'fsdp', split_axis=1, concat_axis=0, tiled=True)  14.5 us
    all_to_all x1, starting transfers between devices, embed_columns(): lax.all_to_all(picked, 'rep', split_axis=0, concat_axis=0, tiled=True)  8.63 us
  transfers between devices with their start and end apart: 6, of which 4 were waited for; matrix products, arithmetic and copies ran while one was open for 20% of the time, Pallas kernels for 0%

commit v1 on v0

v1 whole, which is shorter than its diff:
```python
import functools

import jax
import jax.numpy as jnp
from jax import lax
from jax.experimental import pallas as pl
from jax.experimental.pallas import tpu as pltpu
from jax.sharding import PartitionSpec as P

MIXBITS = 4
EPS = 1e-05
RATE = 0.5
CAP = 32
MESH = pl.DeviceIdType.MESH
F32 = jnp.float32
BF16 = jnp.bfloat16
W_CHUNKS = 4

NT = (((1,), (1,)), ((), ()))
NN = (((1,), (0,)), ((), ()))


def dot(a, b, dims):
    return lax.dot_general(a, b, dims, preferred_element_type=F32)


def kernel(
    level, n_rep, n_fsdp,
    ids_ref, w_ref, h_ref, c_ref, tab_ref, gain_ref, out_ref,
    ids_all, w_own, w_other, heads, heads_t, cot, weighted_t, table, req_out, req_in, picked, fetched, mixed_t,
    stream_t, grad_t, stat_out, stat_in, position_row, gain_col,
    ids_send, ids_recv, w_send, w_recv, h_send, h_recv, c_send, c_recv, req_send, req_recv, row_send, row_recv,
    stat_send, stat_recv, local_sem,
):
    tokens, heads_width = h_ref.shape
    width = w_ref.shape[1]
    rows = w_ref.shape[0]
    features = width * n_fsdp
    all_tokens = tokens * n_fsdp
    vocab = tab_ref.shape[0]
    half = tokens // 2
    chunk = rows // W_CHUNKS
    rep = lax.axis_index("rep")
    me = lax.axis_index("fsdp")
    ring = n_fsdp // 2
    place, core = me // 2, me % 2
    up = (place + 1) % ring * 2 + core
    down = (place + ring - 1) % ring * 2 + core
    across = (place + 2) % ring * 2 + core
    sibling = place * 2 + 1 - core
    stride = 1 << level
    partner = rep + stride * (1 - 2 * (rep // stride % 2))

    def remote(src, dst, send, recv, r, f):
        return pltpu.make_async_remote_copy(
            src_ref=src, dst_ref=dst, send_sem=send, recv_sem=recv, device_id=(r, f), device_id_type=MESH
        )

    own_rows = pl.ds(pl.multiple_of(me * tokens, tokens), tokens)
    local = [
        pltpu.make_async_copy(w_ref, w_own, local_sem.at[0]),
        pltpu.make_async_copy(h_ref, heads.at[own_rows], local_sem.at[1]),
        pltpu.make_async_copy(
            c_ref.at[:, pl.ds(pl.multiple_of(me * width, width), width)], cot.at[me], local_sem.at[2]
        ),
    ]
    for copy in local:
        copy.start()

    barrier = pltpu.get_barrier_semaphore()

    @pl.loop(1, n_fsdp)
    def _(step):
        pl.semaphore_signal(barrier, inc=1, device_id=(rep, (me + step) % n_fsdp), device_id_type=MESH)

    @pl.loop(1, n_rep)
    def _(step):
        pl.semaphore_signal(barrier, inc=1, device_id=((rep + step) % n_rep, me), device_id_type=MESH)

    ids_all[me] = ids_ref[...]
    table[...] = jnp.zeros_like(table)
    table[:vocab] = tab_ref[...]
    gain = gain_ref[:, pl.ds(pl.multiple_of(me * width, width), width)]
    gain_col[...] = jnp.broadcast_to(gain, (128, width)).T

    pl.semaphore_wait(barrier, n_fsdp - 1 + n_rep - 1)

    def ids_copy(step):
        peer = (me + step) % n_fsdp
        return remote(ids_all.at[me], ids_all.at[me], ids_send.at[step], ids_recv.at[me], rep, peer)

    @pl.loop(1, n_fsdp)
    def _(step):
        ids_copy(step).start()

    def w_copy(k):
        part = pl.ds(k * chunk, chunk)
        return remote(w_ref.at[part], w_other.at[part], w_send.at[k], w_recv.at[k], partner, me)

    for k in range(W_CHUNKS):
        w_copy(k).start()

    def part_rows(owner, which):
        return pl.ds(pl.multiple_of(owner * tokens + which * half, half), half)

    def h_copy(index, owner, which, target, own=False):
        src = h_ref.at[pl.ds(which * half, half)] if own else heads.at[part_rows(owner, which)]
        return remote(
            src, heads.at[part_rows(owner, which)], h_send.at[index], h_recv.at[owner, which], rep, target
        )

    def h_wait(owner, which):
        h_copy(0, owner, which, sibling).wait_recv()

    own_sends = [
        h_copy(0, me, 0, up, True),
        h_copy(1, me, 1, down, True),
        h_copy(2, me, 1, up, True),
        h_copy(3, me, 0, down, True),
        h_copy(4, me, 0, sibling, True),
        h_copy(5, me, 1, sibling, True),
    ]
    for copy in own_sends:
        copy.start()

    def c_copy(step):
        peer = (me + step) % n_fsdp
        return remote(
            c_ref.at[:, pl.ds(pl.multiple_of(peer * width, width), width)],
            cot.at[me], c_send.at[step], c_recv.at[me], rep, peer,
        )

    @pl.loop(1, n_fsdp)
    def _(step):
        c_copy(step).start()

    @pl.loop(1, n_fsdp)
    def _(step):
        sender = (me + step) % n_fsdp
        remote(ids_all.at[me], ids_all.at[sender], ids_send.at[step], ids_recv.at[sender], rep, sender).wait_recv()

    ids_row = jnp.concatenate([ids_all[j] for j in range(n_fsdp)], axis=1)
    owner_row = ids_row // vocab
    local_row = ids_row - owner_row * vocab + 1
    block_iota = lax.broadcasted_iota(jnp.int32, (n_rep, all_tokens), 0)
    owned = block_iota == owner_row
    owned_b = jnp.where(owned, 1.0, 0.0).astype(BF16)
    earlier = (
        lax.broadcasted_iota(jnp.int32, (all_tokens, all_tokens), 0)
        < lax.broadcasted_iota(jnp.int32, (all_tokens, all_tokens), 1)
    )
    before = dot(owned_b, jnp.where(earlier, 1.0, 0.0).astype(BF16), NN)
    rank = jnp.sum(jnp.where(owned, before, 0.0), axis=0, keepdims=True).astype(jnp.int32)
    position_row[...] = owner_row * CAP + rank
    per_tile = 128 // CAP
    lane = rank + rep % per_tile * CAP
    here = lax.broadcasted_iota(jnp.int32, (128, all_tokens), 0) == lane
    high = jnp.where(here, (local_row // 2).astype(F32), 0.0).astype(BF16)
    low = jnp.where(here, (local_row % 2).astype(F32), 0.0).astype(BF16)
    requests = dot(owned_b, high, NT) * 2.0 + dot(owned_b, low, NT)
    for v in range(n_rep):
        req_out[v] = requests[v : v + 1]
    req_in[rep] = req_out[rep]

    def req_copy(step):
        peer = (rep + step) % n_rep
        return remote(req_out.at[peer], req_in.at[rep], req_send.at[step], req_recv.at[rep], peer, me)

    @pl.loop(1, n_rep)
    def _(step):
        req_copy(step).start()

    @pl.loop(1, n_rep)
    def _(step):
        sender = (rep + n_rep - step) % n_rep
        remote(req_out.at[sender], req_in.at[sender], req_send.at[step], req_recv.at[sender], sender, me).wait_recv()

    def row_copy(peer):
        return remote(
            picked.at[pl.ds(pl.multiple_of(peer * CAP, CAP), CAP)],
            fetched.at[pl.ds(pl.multiple_of(rep * CAP, CAP), CAP)],
            row_send.at[peer], row_recv.at[rep], peer, me,
        )

    groups = n_rep // per_tile

    @pl.loop(0, groups)
    def _(turn):
        group = (turn + rep // per_tile) % groups
        wanted = req_in[group * per_tile]
        for j in range(1, per_tile):
            wanted = wanted + req_in[group * per_tile + j]
        wanted_col = jnp.broadcast_to(wanted, (128, 128)).T[:, :1]
        hit = lax.broadcasted_iota(jnp.int32, (128, table.shape[0]), 1).astype(F32) + 1.0 == wanted_col
        picked[pl.ds(pl.multiple_of(group * 128, 128), 128)] = dot(
            jnp.where(hit, 1.0, 0.0).astype(BF16), table[...], NN
        ).astype(BF16)
        for j in range(per_tile):
            peer = group * per_tile + j

            @pl.when(peer != rep)
            def _():
                row_copy(peer).start()

    own_slots = pl.ds(pl.multiple_of(rep * CAP, CAP), CAP)
    fetched[own_slots] = picked[own_slots]

    h_wait(down, 0)
    ring_sends = [h_copy(6, down, 0, up), h_copy(7, down, 0, sibling)]
    for copy in ring_sends:
        copy.start()
    h_wait(up, 1)
    more = [h_copy(8, up, 1, down), h_copy(9, up, 1, sibling)]
    for copy in more:
        copy.start()
    ring_sends += more

    def turn_heads(owner):
        for b in range(heads_width // 256):
            block = heads[pl.ds(pl.multiple_of(owner * tokens, tokens), tokens), 256 * b : 256 * (b + 1)]
            heads_t[256 * b : 256 * (b + 1), pl.ds(pl.multiple_of(owner * tokens, tokens), tokens)] = block.T

    for copy in local:
        copy.wait()
    turn_heads(me)

    def turn_cot(owner):
        weighted_t[:, pl.ds(pl.multiple_of(owner * tokens, tokens), tokens)] = (
            cot[owner].astype(F32).T * gain_col[...]
        )

    turn_cot(me)

    h_wait(sibling, 0)
    h_wait(sibling, 1)
    turn_heads(sibling)

    h_wait(down, 1)
    h_wait(up, 0)
    more = [h_copy(10, down, 1, sibling), h_copy(11, up, 0, sibling)]
    for copy in more:
        copy.start()
    ring_sends += more
    turn_heads(down)
    turn_heads(up)

    @pl.loop(1, n_fsdp)
    def _(step):
        sender = (me + step) % n_fsdp
        remote(cot.at[sender], cot.at[sender], c_send.at[step], c_recv.at[sender], rep, sender).wait_recv()
        turn_cot(sender)

    other_up = (place + 1) % ring * 2 + 1 - core
    other_down = (place + ring - 1) % ring * 2 + 1 - core
    other_across = (place + 2) % ring * 2 + 1 - core
    for owner in (other_down, other_up):
        h_wait(owner, 0)
        h_wait(owner, 1)
        turn_heads(owner)
    for which in range(2):
        h_wait(across, which)
        copy = h_copy(12 + which, across, which, sibling)
        copy.start()
        ring_sends.append(copy)
    turn_heads(across)
    h_wait(other_across, 0)
    h_wait(other_across, 1)
    turn_heads(other_across)

    tile = 256
    for k in range(W_CHUNKS):
        w_copy(k).wait_recv()
        part = pl.ds(k * chunk, chunk)
        mixed = (w_own[part].astype(F32) + w_other[part].astype(F32)) * 0.5
        mixed_t[...] = mixed.T.astype(BF16)

        @pl.loop(0, all_tokens // tile)
        def _(i):
            where = pl.ds(pl.multiple_of(i * tile, tile), tile)
            part_sum = dot(mixed_t[...], heads[where, k * chunk : (k + 1) * chunk], NT)
            if k == 0:
                stream_t[:, where] = part_sum
            else:
                stream_t[:, where] += part_sum

    batch = 8
    span = batch * CAP

    @pl.loop(0, n_rep // batch)
    def _(g):
        for j in range(batch):
            v = g * batch + j

            @pl.when(v != rep)
            def _():
                slots = pl.ds(pl.multiple_of(v * CAP, CAP), CAP)
                remote(picked.at[slots], fetched.at[slots], row_send.at[v], row_recv.at[v], v, me).wait_recv()

        slots = pl.ds(pl.multiple_of(g * span, span), span)
        rows_t = fetched[slots].T
        for i in range(all_tokens // tile):
            where = slice(i * tile, (i + 1) * tile)
            slot = lax.broadcasted_iota(jnp.int32, (span, tile), 0) + g * span
            place_of = jnp.where(slot == position_row[:, where], 1.0, 0.0).astype(BF16)
            stream_t[:, where] += dot(rows_t, place_of, NN)

    stream = stream_t[...]
    stat_out[:, :all_tokens] = jnp.sum(stream * stream, axis=0, keepdims=True)
    stat_out[:, all_tokens:] = jnp.sum(stream * weighted_t[...], axis=0, keepdims=True)
    stat_in[me] = stat_out[...]

    def stat_copy(step):
        peer = (me + step) % n_fsdp
        return remote(stat_out, stat_in.at[me], stat_send.at[step], stat_recv.at[me], rep, peer)

    @pl.loop(1, n_fsdp)
    def _(step):
        stat_copy(step).start()

    @pl.loop(1, n_fsdp)
    def _(step):
        sender = (me + step) % n_fsdp
        remote(stat_out, stat_in.at[sender], stat_send.at[step], stat_recv.at[sender], rep, sender).wait_recv()

    total = stat_in[0]
    for j in range(1, n_fsdp):
        total = total + stat_in[j]
    total = total * (1.0 / features)
    inverse = 1.0 / jnp.sqrt(total[:, :all_tokens] + EPS)
    scale = total[:, all_tokens:] * inverse * inverse * inverse
    grad_t[...] = (weighted_t[...] * inverse - stream_t[...] * scale).astype(BF16)

    @pl.loop(0, rows // tile)
    def _(i):
        where = pl.ds(pl.multiple_of(i * tile, tile), tile)
        grad = dot(heads_t[where], grad_t[...], NT)
        mixed = (w_own[where].astype(F32) + w_other[where].astype(F32)) * 0.5
        out_ref[where] = (mixed - (RATE / all_tokens) * grad).astype(BF16)

    for copy in own_sends + ring_sends:
        copy.wait_send()
    for k in range(W_CHUNKS):
        w_copy(k).wait_send()

    @pl.loop(1, n_fsdp)
    def _(step):
        ids_copy(step).wait_send()
        c_copy(step).wait_send()
        stat_copy(step).wait_send()

    @pl.loop(1, n_rep)
    def _(step):
        req_copy(step).wait_send()
        row_copy((rep + step) % n_rep).wait_send()


def make_branch(level, n_rep, n_fsdp, weights, head_out, embed_table):
    rows, width = weights.shape
    tokens, heads_width = head_out.shape
    all_tokens = tokens * n_fsdp
    vocab_pad = -(-embed_table.shape[0] // 256) * 256
    dma = pltpu.SemaphoreType.DMA
    vmem = pl.BlockSpec(memory_space=pltpu.VMEM)
    hbm = pl.BlockSpec(memory_space=pl.ANY)
    slots = n_rep * CAP
    return pl.pallas_call(
        functools.partial(kernel, level, n_rep, n_fsdp),
        name=f"step_level_{level}",
        out_shape=jax.ShapeDtypeStruct((rows, width), BF16),
        in_specs=[vmem, hbm, hbm, hbm, vmem, vmem],
        out_specs=vmem,
        scratch_shapes=[
            pltpu.VMEM((n_fsdp, 1, tokens), jnp.int32),
            pltpu.VMEM((rows, width), BF16),
            pltpu.VMEM((rows, width), BF16),
            pltpu.VMEM((all_tokens, heads_width), BF16),
            pltpu.VMEM((heads_width, all_tokens), BF16),
            pltpu.VMEM((n_fsdp, tokens, width), BF16),
            pltpu.VMEM((width, all_tokens), F32),
            pltpu.VMEM((vocab_pad, width), BF16),
            pltpu.VMEM((n_rep, 1, 128), F32),
            pltpu.VMEM((n_rep, 1, 128), F32),
            pltpu.VMEM((slots, width), BF16),
            pltpu.VMEM((slots, width), BF16),
            pltpu.VMEM((width, rows // W_CHUNKS), BF16),
            pltpu.VMEM((width, all_tokens), F32),
            pltpu.VMEM((width, all_tokens), BF16),
            pltpu.VMEM((1, 2 * all_tokens), F32),
            pltpu.VMEM((n_fsdp, 1, 2 * all_tokens), F32),
            pltpu.VMEM((1, all_tokens), jnp.int32),
            pltpu.VMEM((width, 128), F32),
            dma((n_fsdp,)), dma((n_fsdp,)),
            dma((W_CHUNKS,)), dma((W_CHUNKS,)),
            dma((14,)), dma((n_fsdp, 2)),
            dma((n_fsdp,)), dma((n_fsdp,)),
            dma((n_rep,)), dma((n_rep,)),
            dma((n_rep,)), dma((n_rep,)),
            dma((n_fsdp,)), dma((n_fsdp,)),
            dma((3,)),
        ],
        compiler_params=pltpu.CompilerParams(
            collective_id=level, has_side_effects=True, vmem_limit_bytes=44 * 1024 * 1024
        ),
        cost_estimate=pl.CostEstimate(
            flops=6 * rows * width * all_tokens, bytes_accessed=8 * rows * width, transcendentals=all_tokens
        ),
    )


def local(weights, head_out, token_ids, embed_table, norm_gain, cotangent, mix_step):
    n_rep, n_fsdp = lax.axis_size("rep"), lax.axis_size("fsdp")
    branches = [
        make_branch(level, n_rep, n_fsdp, weights[0], head_out[0], embed_table) for level in range(MIXBITS)
    ]
    out = lax.switch(
        mix_step[0] % MIXBITS,
        branches,
        token_ids, weights[0], head_out[0], cotangent[0], embed_table, norm_gain[None],
    )
    return out[None]


def solution(mesh):
    return jax.shard_map(
        local,
        mesh=mesh,
        in_specs=(
            P("rep", None, "fsdp"),
            P("rep", "fsdp", None),
            P("rep", "fsdp"),
            P("rep", "fsdp"),
            P(),
            P("rep", "fsdp", None),
            P(),
        ),
        out_specs=P("rep", None, "fsdp"),
        check_vma=False,
    )
```

time: 247 us -> 105 us (0.43)
  Pallas kernels: 0 us -> 102 us
  waiting for transfers between devices: 84.5 us -> 0 us
  blocking collectives: 60.3 us -> 0 us
  starting transfers between devices: 26.6 us -> 0 us
  local copies, waits for them, and re-layouts: 27.1 us -> 1.65 us
  other arithmetic: 22.8 us -> 0 us
  between operations: 14.3 us -> 0.69 us
  matrix products: 9.98 us -> 0 us
    pallas_call x0 -> x1, Pallas kernels: none -> 102 us  [local(): lax.switch(mix_step[0] % MIXBITS, branches, token_ids, weights[0], head_o...]
    all_to_all x3 -> x0, waiting for transfers between devices: 65.5 us -> none  [the longest x1 27 us: embed_columns(): lax.all_to_all(picked, 'rep', split_axis=0, concat_axis=0, tiled=True)]
    all_to_all x1 -> x0, blocking collectives: 36.5 us -> none  [embed_columns(): lax.all_to_all(requests, 'rep', split_axis=0, concat_axis=0, tiled=True)]
    all_gather x1 -> x0, blocking collectives: 23.8 us -> none  [embed_columns(): replica_ids = lax.all_gather(token_ids, 'fsdp', axis=1, tiled=True)[0]]
    all_to_all x3 -> x0, starting transfers between devices: 22.6 us -> none  [the longest x1 8.63 us: embed_columns(): lax.all_to_all(picked, 'rep', split_axis=0, concat_axis=0, tiled=True)]
    ppermute x1 -> x0, waiting for transfers between devices: 18.3 us -> none  [partner(): return lax.ppermute(block, axis, route)]
    another operation x2 -> x0, other arithmetic: 18 us -> none
    gather x2 -> x0, local copies, waits for them, and re-layouts: 12.5 us -> none  [the longest x1 7.5 us: embed_columns(): jnp.take(embed_table, jnp.clip(requested, 0, rows_each - 1), axis=0)]
  transfers between devices with their start and end apart: 6 -> 0, of which waited for: 4 -> 0; matrix products, arithmetic and copies ran while one was open for 20% -> 0% of each run, Pallas kernels for 0% -> 0%
where the time goes in v1:
time: 105 us; the launch traced here: 104 us
  Pallas kernels  102 us (97%)
  local copies, waits for them, and re-layouts  1.65 us (2%)
    pallas_call x1, Pallas kernels, local(): lax.switch(mix_step[0] % MIXBITS, branches, token_ids, weights[0], head_o...  102 us

profile of v1, /device:TPU:1, one launch (start us, length us, event | category | flops | bytes accessed | tf_op | source)
XLA Modules:
  0.0 104.4 jit_solution(9434555051101514324)
XLA Ops:
  0.7 0.0 copy-start
  0.7 0.0 copy-start.1
  0.7 0.7 copy-done
  1.4 0.0 copy-done.1
  1.4 102.0 %conditional.1 = (bf16[1,2048,256]{2,1,0:T(8,128)(2,1)S(1)}) conditional(s32[]{:T(128)} %clamp.3, (s32[1,128]{1,0:T(1,128)S(1)}, bf16[2048,256]{1,0:T(8,128)(2,1)}, bf16[128,2048]{1,0:T(8,128)(2,1)}, bf16[128,2048]{1,0:T(8,128)(2,1)}, bf16[500,256]{1,0:T(8,128)(2,1)}, /*index=5*/f32[1,2048]{1,0:T(1,128)S(1)}) %tuple.46, ...), branch_computations={%region_0.1_spmd, %region_1.2_spmd, %region_2.3_spmd, %region_3.4_... | conditional | flops 3221225472 | bytes 4194312 | solution.py:415
  1.4 101.8 %step_level_0.1 = bf16[2048,256]{1,0:T(8,128)(2,1)S(1)} custom-call(s32[1,128]{1,0:T(1,128)S(1)} %get-tuple-element.58.ids_ref, bf16[2048,256]{1,0:T(8,128)(2,1)} %get-tuple-element.60.w_ref, bf16[128,2048]{1,0:T(8,128)(2,1)} %get-tuple-element.61.h_ref, bf16[128,2048]{1,0:T(8,128)(2,1)} %get-tuple-element.62.c_ref, ...), custom_call_target="tpu_custom_call" | custom-call | flops 3221225472 | bytes 4194304 | tf_op jit(solution)/shard_map/cond/branch_0_fun/step_level_0/pallas_call | solution.py:415
  103.4 1.0 copy.18
Async XLA Ops:
  0.7 0.7 copy-start
  0.7 0.7 copy-start.1

commit v2 on v1

v2 whole, which is shorter than its diff:
```python
import functools

import jax
import jax.numpy as jnp
from jax import lax
from jax.experimental import pallas as pl
from jax.experimental.pallas import tpu as pltpu
from jax.sharding import PartitionSpec as P

MIXBITS = 4
EPS = 1e-05
RATE = 0.5
CAP = 32
MESH = pl.DeviceIdType.MESH
F32 = jnp.float32
BF16 = jnp.bfloat16
W_CHUNKS = 8
W_FIRST = 2
W_NEXT = 2

NT = (((1,), (1,)), ((), ()))
NN = (((1,), (0,)), ((), ()))


def dot(a, b, dims):
    return lax.dot_general(a, b, dims, preferred_element_type=F32)


def kernel(
    level, n_rep, n_fsdp,
    ids_ref, w_ref, h_ref, c_ref, tab_ref, gain_ref, out_ref,
    ids_all, w_own, w_other, heads, heads_t, cot, weighted_t, table, req_out, req_in, picked, fetched, mixed_t,
    stream_t, grad_t, stat_out, stat_in, gain_col, place_of,
    ids_send, ids_recv, w_send, w_recv, h_send, h_recv, c_send, c_recv, req_send, req_recv, row_send, row_recv,
    stat_send, stat_recv, local_sem, out_sem,
):
    tokens, heads_width = h_ref.shape
    width = w_ref.shape[1]
    rows = w_ref.shape[0]
    features = width * n_fsdp
    all_tokens = tokens * n_fsdp
    vocab = tab_ref.shape[0]
    half = tokens // 2
    chunk = rows // W_CHUNKS
    rep = lax.axis_index("rep")
    me = lax.axis_index("fsdp")
    ring = n_fsdp // 2
    place, core = me // 2, me % 2
    up = (place + 1) % ring * 2 + core
    down = (place + ring - 1) % ring * 2 + core
    across = (place + 2) % ring * 2 + core
    sibling = place * 2 + 1 - core
    stride = 1 << level
    partner = rep + stride * (1 - 2 * (rep // stride % 2))

    def remote(src, dst, send, recv, r, f):
        return pltpu.make_async_remote_copy(
            src_ref=src, dst_ref=dst, send_sem=send, recv_sem=recv, device_id=(r, f), device_id_type=MESH
        )

    own_rows = pl.ds(pl.multiple_of(me * tokens, tokens), tokens)
    local = [
        pltpu.make_async_copy(w_ref, w_own, local_sem.at[0]),
        pltpu.make_async_copy(h_ref, heads.at[own_rows], local_sem.at[1]),
        pltpu.make_async_copy(
            c_ref.at[:, pl.ds(pl.multiple_of(me * width, width), width)], cot.at[me], local_sem.at[2]
        ),
    ]
    for copy in local:
        copy.start()

    barrier = pltpu.get_barrier_semaphore()

    @pl.loop(1, n_fsdp)
    def _(step):
        pl.semaphore_signal(barrier, inc=1, device_id=(rep, (me + step) % n_fsdp), device_id_type=MESH)

    @pl.loop(1, n_rep)
    def _(step):
        pl.semaphore_signal(barrier, inc=1, device_id=((rep + step) % n_rep, me), device_id_type=MESH)

    ids_all[me] = ids_ref[...]
    table[...] = jnp.zeros_like(table)
    table[:vocab] = tab_ref[...]
    gain = gain_ref[:, pl.ds(pl.multiple_of(me * width, width), width)]
    gain_col[...] = jnp.broadcast_to(gain, (128, width)).T

    pl.semaphore_wait(barrier, n_fsdp - 1 + n_rep - 1)

    def ids_copy(step):
        peer = (me + step) % n_fsdp
        return remote(ids_all.at[me], ids_all.at[me], ids_send.at[step], ids_recv.at[me], rep, peer)

    @pl.loop(1, n_fsdp)
    def _(step):
        ids_copy(step).start()

    def w_copy(k):
        part = pl.ds(k * chunk, chunk)
        return remote(w_ref.at[part], w_other.at[part], w_send.at[k], w_recv.at[k], partner, me)

    for k in range(W_FIRST):
        w_copy(k).start()

    def part_rows(owner, which):
        return pl.ds(pl.multiple_of(owner * tokens + which * half, half), half)

    def h_copy(index, owner, which, target, own=False):
        src = h_ref.at[pl.ds(which * half, half)] if own else heads.at[part_rows(owner, which)]
        return remote(
            src, heads.at[part_rows(owner, which)], h_send.at[index], h_recv.at[owner, which], rep, target
        )

    def h_wait(owner, which):
        h_copy(0, owner, which, sibling).wait_recv()

    own_sends = [
        h_copy(0, me, 0, up, True),
        h_copy(1, me, 1, down, True),
        h_copy(2, me, 1, up, True),
        h_copy(3, me, 0, down, True),
        h_copy(4, me, 0, sibling, True),
        h_copy(5, me, 1, sibling, True),
    ]
    for copy in own_sends[:2]:
        copy.start()

    def c_copy(step):
        peer = (me + step) % n_fsdp
        return remote(
            c_ref.at[:, pl.ds(pl.multiple_of(peer * width, width), width)],
            cot.at[me], c_send.at[step], c_recv.at[me], rep, peer,
        )

    earlier = jnp.where(
        lax.broadcasted_iota(jnp.int32, (tokens, tokens), 0) < lax.broadcasted_iota(jnp.int32, (tokens, tokens), 1),
        1.0,
        0.0,
    ).astype(BF16)

    def start_c():
        @pl.loop(1, n_fsdp)
        def _(step):
            c_copy(step).start()

    ring_sends = []

    def pass_on(*copies):
        for copy in copies:
            copy.start()
            ring_sends.append(copy)

    def forward():
        h_wait(down, 0)
        pass_on(h_copy(6, down, 0, up), h_copy(7, down, 0, sibling))
        h_wait(up, 1)
        pass_on(h_copy(8, up, 1, down), h_copy(9, up, 1, sibling))

    @pl.loop(1, n_fsdp)
    def _(step):
        sender = (me + step) % n_fsdp
        remote(ids_all.at[me], ids_all.at[sender], ids_send.at[step], ids_recv.at[sender], rep, sender).wait_recv()

    ids_row = jnp.concatenate([ids_all[j] for j in range(n_fsdp)], axis=1)
    owner_row = ids_row // vocab
    local_row = ids_row - owner_row * vocab + 1
    block_iota = lax.broadcasted_iota(jnp.int32, (n_rep, all_tokens), 0)
    owned = block_iota == owner_row
    owned_b = jnp.where(owned, 1.0, 0.0).astype(BF16)
    ranks = []
    seen = jnp.zeros((n_rep, 1), F32)
    for j in range(n_fsdp):
        part = slice(j * tokens, (j + 1) * tokens)
        before = dot(owned_b[:, part], earlier, NN) + seen
        ranks.append(jnp.sum(jnp.where(owned[:, part], before, 0.0), axis=0, keepdims=True))
        seen = seen + jnp.sum(jnp.where(owned[:, part], 1.0, 0.0), axis=1, keepdims=True)
    rank = jnp.concatenate(ranks, axis=1).astype(jnp.int32)
    position = owner_row * CAP + rank
    per_tile = 128 // CAP
    lane = rank + rep % per_tile * CAP
    here = lax.broadcasted_iota(jnp.int32, (128, all_tokens), 0) == lane
    high = jnp.where(here, (local_row // 2).astype(F32), 0.0).astype(BF16)
    low = jnp.where(here, (local_row % 2).astype(F32), 0.0).astype(BF16)
    counted = dot(owned_b, jnp.concatenate([high, low], axis=0), NT)
    requests = counted[:, :128] * 2.0 + counted[:, 128:]
    for v in range(n_rep):
        req_out[v] = requests[v : v + 1]
    req_in[rep] = req_out[rep]

    pair = 2 * per_tile
    pairs = n_rep // pair

    def req_copy(step):
        peer = (rep // pair + step // pair) % pairs * pair + (rep + step) % pair
        return remote(req_out.at[peer], req_in.at[rep], req_send.at[step], req_recv.at[rep], peer, me)

    @pl.loop(1, n_rep)
    def _(step):
        req_copy(step).start()

    for k in range(W_FIRST, W_FIRST + W_NEXT):
        w_copy(k).start()

    for copy in own_sends[2:]:
        copy.start()
    start_c()
    forward()

    def row_copy(peer):
        return remote(
            picked.at[pl.ds(pl.multiple_of(peer * CAP, CAP), CAP)],
            fetched.at[pl.ds(pl.multiple_of(rep * CAP, CAP), CAP)],
            row_send.at[peer], row_recv.at[rep], peer, me,
        )

    @pl.loop(0, pairs)
    def _(turn):
        first = (rep // pair + pairs - turn) % pairs * pair
        for j in range(pair):
            sender = first + (rep + j) % pair

            @pl.when(sender != rep)
            def _():
                remote(
                    req_out.at[sender], req_in.at[sender], req_send.at[0], req_recv.at[sender], sender, me
                ).wait_recv()

        columns = []
        for g in range(2):
            wanted = req_in[first + g * per_tile]
            for j in range(1, per_tile):
                wanted = wanted + req_in[first + g * per_tile + j]
            columns.append(jnp.broadcast_to(wanted, (8, 128)).T[:, :1])
        wanted_col = jnp.concatenate(columns, axis=0)
        hit = lax.broadcasted_iota(jnp.int32, (256, table.shape[0]), 1).astype(F32) + 1.0 == wanted_col
        picked[pl.ds(pl.multiple_of(first * CAP, 256), 256)] = dot(
            jnp.where(hit, 1.0, 0.0).astype(BF16), table[...], NN
        ).astype(BF16)
        for j in range(pair):
            peer = first + (rep + j) % pair

            @pl.when(peer != rep)
            def _():
                row_copy(peer).start()

    for k in range(W_FIRST + W_NEXT, W_CHUNKS):
        w_copy(k).start()

    own_slots = pl.ds(pl.multiple_of(rep * CAP, CAP), CAP)
    fetched[own_slots] = picked[own_slots]

    tile = 256
    for copy in local:
        copy.wait()

    @pl.loop(0, n_rep * CAP // tile)
    def _(i):
        slot = lax.broadcasted_iota(jnp.int32, (tile, all_tokens), 0) + i * tile
        place_of[pl.ds(pl.multiple_of(i * tile, tile), tile)] = jnp.where(slot == position, 1.0, 0.0).astype(BF16)

    def token_rows(owner):
        return pl.ds(pl.multiple_of(owner * tokens, tokens), tokens)

    def turn_heads(owner):
        for b in range(heads_width // 256):
            heads_t[256 * b : 256 * (b + 1), token_rows(owner)] = heads[
                token_rows(owner), 256 * b : 256 * (b + 1)
            ].T

    def turn_cot(owner):
        weighted_t[:, token_rows(owner)] = cot[owner].astype(F32).T * gain_col[...]

    def embed(begin, end):
        @pl.loop(begin, end)
        def _(turn):
            first = (rep // pair + turn) % pairs * pair
            for j in range(pair):
                v = first + j

                @pl.when(v != rep)
                def _():
                    slots = pl.ds(pl.multiple_of(v * CAP, CAP), CAP)
                    remote(
                        picked.at[slots], fetched.at[slots], row_send.at[v], row_recv.at[v], v, me
                    ).wait_recv()

            slots = pl.ds(pl.multiple_of(first * CAP, pair * CAP), pair * CAP)
            rows_t = fetched[slots].T
            stream_t[...] += dot(rows_t, place_of[slots], NN)

    def mix(k):
        w_copy(k).wait_recv()
        part = pl.ds(k * chunk, chunk)
        mixed = (w_own[part].astype(F32) + w_other[part].astype(F32)) * 0.5
        mixed_t[:, part] = mixed.astype(BF16).T

    def project(k, count=1):
        part = slice(k * chunk, (k + count) * chunk)
        stream_t[...] += dot(mixed_t[:, part], heads_t[part], NN)

    def project_place(at):
        where = pl.ds(pl.multiple_of(at * 2 * tokens, 2 * tokens), 2 * tokens)
        stream_t[:, where] += dot(mixed_t[...], heads_t[:, where], NN)

    other_up = (place + 1) % ring * 2 + 1 - core
    other_down = (place + ring - 1) % ring * 2 + 1 - core
    other_across = (place + 2) % ring * 2 + 1 - core

    def finish_sends():
        @pl.loop(1, n_fsdp)
        def _(step):
            ids_copy(step).wait_send()
            c_copy(step).wait_send()

        @pl.loop(1, n_rep)
        def _(step):
            req_copy(step).wait_send()
            row_copy((rep + step) % n_rep).wait_send()

        for k in range(W_CHUNKS):
            w_copy(k).wait_send()

    stream_t[...] = jnp.zeros_like(stream_t)
    turn_heads(me)
    turn_cot(me)
    h_wait(sibling, 0)
    h_wait(sibling, 1)
    turn_heads(sibling)
    h_wait(down, 1)
    h_wait(up, 0)
    pass_on(h_copy(10, down, 1, sibling), h_copy(11, up, 0, sibling))
    turn_heads(down)
    turn_heads(up)
    for owner in (other_down, other_up):
        h_wait(owner, 0)
        h_wait(owner, 1)
        turn_heads(owner)

    @pl.loop(1, n_fsdp)
    def _(step):
        sender = (me + step) % n_fsdp
        remote(cot.at[sender], cot.at[sender], c_send.at[step], c_recv.at[sender], rep, sender).wait_recv()
        turn_cot(sender)

    def take_across():
        for which in range(2):
            h_wait(across, which)
            pass_on(h_copy(12 + which, across, which, sibling))
        turn_heads(across)
        h_wait(other_across, 0)
        h_wait(other_across, 1)
        turn_heads(other_across)

    late = pairs - 2
    early = W_FIRST + W_NEXT
    if level == 0:
        for k in range(W_CHUNKS):
            mix(k)
        for step in (0, 1, ring - 1):
            project_place((place + step) % ring)
        embed(0, late)
        take_across()
        project_place((place + 2) % ring)
        finish_sends()
        embed(late, pairs)
    else:
        for k in range(early):
            mix(k)
        embed(0, late)
        take_across()
        project(0, early)
        embed(late, pairs)
        for k in range(early, W_CHUNKS - 1):
            mix(k)
            project(k)
        finish_sends()
        mix(W_CHUNKS - 1)
        project(W_CHUNKS - 1)

    stream = stream_t[...]
    stat_out[:, :all_tokens] = jnp.sum(stream * stream, axis=0, keepdims=True)
    stat_out[:, all_tokens:] = jnp.sum(stream * weighted_t[...], axis=0, keepdims=True)

    def stat_copy(step):
        peer = (me + step) % n_fsdp
        return remote(stat_out, stat_in.at[me], stat_send.at[step], stat_recv.at[me], rep, peer)

    for step in range(1, n_fsdp):
        stat_copy(step).start()
    stat_in[me] = stat_out[...]
    for step in range(1, n_fsdp):
        sender = (me + step) % n_fsdp
        remote(stat_out, stat_in.at[sender], stat_send.at[step], stat_recv.at[sender], rep, sender).wait_recv()

    total = stat_in[0]
    for j in range(1, n_fsdp):
        total = total + stat_in[j]
    total = total * (1.0 / features)
    inverse = 1.0 / jnp.sqrt(total[:, :all_tokens] + EPS)
    scale = total[:, all_tokens:] * inverse * inverse * inverse
    grad_t[...] = (weighted_t[...] * inverse - stream_t[...] * scale).astype(BF16)

    @pl.loop(0, rows // (2 * tile))
    def _(i):
        where = pl.ds(pl.multiple_of(i * 2 * tile, 2 * tile), 2 * tile)
        grad = dot(heads_t[where], grad_t[...], NT)
        mixed = (w_own[where].astype(F32) + w_other[where].astype(F32)) * 0.5
        w_own[where] = (mixed - (RATE / all_tokens) * grad).astype(BF16)
        pltpu.make_async_copy(w_own.at[where], out_ref.at[where], out_sem.at[i]).start()

    for i in range(rows // (2 * tile)):
        where = pl.ds(i * 2 * tile, 2 * tile)
        pltpu.make_async_copy(w_own.at[where], out_ref.at[where], out_sem.at[i]).wait()
    for copy in own_sends + ring_sends:
        copy.wait_send()
    for step in range(1, n_fsdp):
        stat_copy(step).wait_send()


def make_branch(level, n_rep, n_fsdp, weights, head_out, embed_table):
    rows, width = weights.shape
    tokens, heads_width = head_out.shape
    all_tokens = tokens * n_fsdp
    vocab_pad = -(-embed_table.shape[0] // 256) * 256
    dma = pltpu.SemaphoreType.DMA
    vmem = pl.BlockSpec(memory_space=pltpu.VMEM)
    hbm = pl.BlockSpec(memory_space=pl.ANY)
    slots = n_rep * CAP
    return pl.pallas_call(
        functools.partial(kernel, level, n_rep, n_fsdp),
        name=f"step_level_{level}",
        out_shape=jax.ShapeDtypeStruct((rows, width), BF16),
        in_specs=[vmem, hbm, hbm, hbm, vmem, vmem],
        out_specs=hbm,
        scratch_shapes=[
            pltpu.VMEM((n_fsdp, 1, tokens), jnp.int32),
            pltpu.VMEM((rows, width), BF16),
            pltpu.VMEM((rows, width), BF16),
            pltpu.VMEM((all_tokens, heads_width), BF16),
            pltpu.VMEM((heads_width, all_tokens), BF16),
            pltpu.VMEM((n_fsdp, tokens, width), BF16),
            pltpu.VMEM((width, all_tokens), F32),
            pltpu.VMEM((vocab_pad, width), BF16),
            pltpu.VMEM((n_rep, 1, 128), F32),
            pltpu.VMEM((n_rep, 1, 128), F32),
            pltpu.VMEM((slots, width), BF16),
            pltpu.VMEM((slots, width), BF16),
            pltpu.VMEM((width, rows), BF16),
            pltpu.VMEM((width, all_tokens), F32),
            pltpu.VMEM((width, all_tokens), BF16),
            pltpu.VMEM((1, 2 * all_tokens), F32),
            pltpu.VMEM((n_fsdp, 1, 2 * all_tokens), F32),
            pltpu.VMEM((width, 128), F32),
            pltpu.VMEM((slots, all_tokens), BF16),
            dma((n_fsdp,)), dma((n_fsdp,)),
            dma((W_CHUNKS,)), dma((W_CHUNKS,)),
            dma((14,)), dma((n_fsdp, 2)),
            dma((n_fsdp,)), dma((n_fsdp,)),
            dma((n_rep,)), dma((n_rep,)),
            dma((n_rep,)), dma((n_rep,)),
            dma((n_fsdp,)), dma((n_fsdp,)),
            dma((3,)), dma((rows // 512,)),
        ],
        compiler_params=pltpu.CompilerParams(
            collective_id=level, has_side_effects=True, vmem_limit_bytes=44 * 1024 * 1024
        ),
        cost_estimate=pl.CostEstimate(
            flops=6 * rows * width * all_tokens, bytes_accessed=8 * rows * width, transcendentals=all_tokens
        ),
    )


def local(weights, head_out, token_ids, embed_table, norm_gain, cotangent, mix_step):
    n_rep, n_fsdp = lax.axis_size("rep"), lax.axis_size("fsdp")
    branches = [
        make_branch(level, n_rep, n_fsdp, weights[0], head_out[0], embed_table) for level in range(MIXBITS)
    ]
    out = lax.switch(
        mix_step[0] % MIXBITS,
        branches,
        token_ids, weights[0], head_out[0], cotangent[0], embed_table, norm_gain[None],
    )
    return out[None]


def solution(mesh):
    return jax.shard_map(
        local,
        mesh=mesh,
        in_specs=(
            P("rep", None, "fsdp"),
            P("rep", "fsdp", None),
            P("rep", "fsdp"),
            P("rep", "fsdp"),
            P(),
            P("rep", "fsdp", None),
            P(),
        ),
        out_specs=P("rep", None, "fsdp"),
        check_vma=False,
    )
```

time: 105 us -> 106 us (level)
  the two profiles are of different devices: /device:TPU:1 before, /device:TPU:57 now
where the time goes in v2:
time: 106 us; the launch traced here: 105 us
  Pallas kernels  103 us (97%)
  local copies, waits for them, and re-layouts  1.65 us (2%)
    pallas_call x1, Pallas kernels, local(): lax.switch(mix_step[0] % MIXBITS, branches, token_ids, weights[0], head_o...  103 us

profile of v2, /device:TPU:57, one launch (start us, length us, event | category | flops | bytes accessed | tf_op | source)
XLA Modules:
  0.0 105.4 jit_solution(15666529448389941951)
XLA Ops:
  0.7 0.0 copy-start
  0.7 0.0 copy-start.1
  0.7 0.7 copy-done
  1.4 0.0 copy-done.1
  1.4 103.0 %conditional.1 = (bf16[1,2048,256]{2,1,0:T(8,128)(2,1)S(1)}) conditional(s32[]{:T(128)} %clamp.3, (s32[1,128]{1,0:T(1,128)S(1)}, bf16[2048,256]{1,0:T(8,128)(2,1)}, bf16[128,2048]{1,0:T(8,128)(2,1)}, bf16[128,2048]{1,0:T(8,128)(2,1)}, bf16[500,256]{1,0:T(8,128)(2,1)}, /*index=5*/f32[1,2048]{1,0:T(1,128)S(1)}) %tuple.46, ...), branch_computations={%region_0.1_spmd, %region_1.2_spmd, %region_2.3_spmd, %region_3.4_... | conditional | flops 3221225472 | bytes 4194312 | solution.py:478
  1.4 103.0 %step_level_2.1 = bf16[2048,256]{1,0:T(8,128)(2,1)S(1)} custom-call(s32[1,128]{1,0:T(1,128)S(1)} %get-tuple-element.71.ids_ref, bf16[2048,256]{1,0:T(8,128)(2,1)} %get-tuple-element.72.w_ref, bf16[128,2048]{1,0:T(8,128)(2,1)} %get-tuple-element.73.h_ref, bf16[128,2048]{1,0:T(8,128)(2,1)} %get-tuple-element.74.c_ref, ...), custom_call_target="tpu_custom_call" | custom-call | flops 3221225472 | bytes 4194304 | tf_op jit(solution)/shard_map/cond/branch_2_fun/step_level_2/pallas_call | solution.py:478
  104.4 1.0 copy.18
Async XLA Ops:
  0.7 0.7 copy-start
  0.7 0.7 copy-start.1

commit v3 on v2

--- a/solution.py
+++ b/solution.py
@@ -10,13 +10,13 @@
 MIXBITS = 4
 EPS = 1e-05
 RATE = 0.5
+PLACES = 8
 CAP = 32
 MESH = pl.DeviceIdType.MESH
 F32 = jnp.float32
 BF16 = jnp.bfloat16
 W_CHUNKS = 8
-W_FIRST = 2
-W_NEXT = 2
+W_SENT = ((2, 6), (3, 3), (3, 3), (3, 3))
 
 NT = (((1,), (1,)), ((), ()))
 NN = (((1,), (0,)), ((), ()))
@@ -32,7 +32,7 @@
     ids_all, w_own, w_other, heads, heads_t, cot, weighted_t, table, req_out, req_in, picked, fetched, mixed_t,
     stream_t, grad_t, stat_out, stat_in, gain_col, place_of,
     ids_send, ids_recv, w_send, w_recv, h_send, h_recv, c_send, c_recv, req_send, req_recv, row_send, row_recv,
-    stat_send, stat_recv, local_sem, out_sem,
+    stat_send, stat_recv, local_sem, out_sem, table_send, table_recv,
 ):
     tokens, heads_width = h_ref.shape
     width = w_ref.shape[1]
@@ -50,7 +50,16 @@
     down = (place + ring - 1) % ring * 2 + core
     across = (place + 2) % ring * 2 + core
     sibling = place * 2 + 1 - core
+    side = rep // PLACES % 2
+    across_z = rep + PLACES * (1 - 2 * side)
+    n_peers = n_rep // 2
+    my = rep // (2 * PLACES) * PLACES + rep % PLACES
+
+    def replica(index):
+        return index // PLACES * (2 * PLACES) + side * PLACES + index % PLACES
+
     stride = 1 << level
+    w_first, w_next = W_SENT[level]
     partner = rep + stride * (1 - 2 * (rep // stride % 2))
 
     def remote(src, dst, send, recv, r, f):
@@ -75,17 +84,19 @@
     def _(step):
         pl.semaphore_signal(barrier, inc=1, device_id=(rep, (me + step) % n_fsdp), device_id_type=MESH)
 
-    @pl.loop(1, n_rep)
+    @pl.loop(1, n_peers)
     def _(step):
-        pl.semaphore_signal(barrier, inc=1, device_id=((rep + step) % n_rep, me), device_id_type=MESH)
+        pl.semaphore_signal(barrier, inc=1, device_id=(replica((my + step) % n_peers), me), device_id_type=MESH)
+
+    pl.semaphore_signal(barrier, inc=1, device_id=(across_z, me), device_id_type=MESH)
 
     ids_all[me] = ids_ref[...]
-    table[...] = jnp.zeros_like(table)
-    table[:vocab] = tab_ref[...]
+    table[side] = jnp.zeros(table.shape[1:], BF16)
+    table[side, :vocab] = tab_ref[...]
     gain = gain_ref[:, pl.ds(pl.multiple_of(me * width, width), width)]
     gain_col[...] = jnp.broadcast_to(gain, (128, width)).T
 
-    pl.semaphore_wait(barrier, n_fsdp - 1 + n_rep - 1)
+    pl.semaphore_wait(barrier, n_fsdp - 1 + n_peers)
 
     def ids_copy(step):
         peer = (me + step) % n_fsdp
@@ -95,11 +106,14 @@
     def _(step):
         ids_copy(step).start()
 
+    table_copy = remote(table.at[side], table.at[side], table_send.at[0], table_recv.at[0], across_z, me)
+    table_copy.start()
+
     def w_copy(k):
         part = pl.ds(k * chunk, chunk)
         return remote(w_ref.at[part], w_other.at[part], w_send.at[k], w_recv.at[k], partner, me)
 
-    for k in range(W_FIRST):
+    for k in range(w_first):
         w_copy(k).start()
 
     def part_rows(owner, which):
@@ -175,30 +189,33 @@
         ranks.append(jnp.sum(jnp.where(owned[:, part], before, 0.0), axis=0, keepdims=True))
         seen = seen + jnp.sum(jnp.where(owned[:, part], 1.0, 0.0), axis=1, keepdims=True)
     rank = jnp.concatenate(ranks, axis=1).astype(jnp.int32)
-    position = owner_row * CAP + rank
-    per_tile = 128 // CAP
-    lane = rank + rep % per_tile * CAP
+    owner_side = owner_row // PLACES % 2
+    owner_peer = owner_row // (2 * PLACES) * PLACES + owner_row % PLACES
+    position = (owner_peer * 2 + owner_side) * CAP + rank
+    asked = lax.broadcasted_iota(jnp.int32, (n_peers, all_tokens), 0) == owner_peer
+    asked_b = jnp.where(asked, 1.0, 0.0).astype(BF16)
+    lane = (owner_side * 2 + my % 2) * CAP + rank
     here = lax.broadcasted_iota(jnp.int32, (128, all_tokens), 0) == lane
     high = jnp.where(here, (local_row // 2).astype(F32), 0.0).astype(BF16)
     low = jnp.where(here, (local_row % 2).astype(F32), 0.0).astype(BF16)
-    counted = dot(owned_b, jnp.concatenate([high, low], axis=0), NT)
+    counted = dot(asked_b, jnp.concatenate([high, low], axis=0), NT)
     requests = counted[:, :128] * 2.0 + counted[:, 128:]
-    for v in range(n_rep):
+    for v in range(n_peers):
         req_out[v] = requests[v : v + 1]
-    req_in[rep] = req_out[rep]
-
-    pair = 2 * per_tile
-    pairs = n_rep // pair
+    req_in[my] = req_out[my]
+
+    pair = PLACES
+    pairs = n_peers // pair
 
     def req_copy(step):
-        peer = (rep // pair + step // pair) % pairs * pair + (rep + step) % pair
-        return remote(req_out.at[peer], req_in.at[rep], req_send.at[step], req_recv.at[rep], peer, me)
-
-    @pl.loop(1, n_rep)
+        peer = (my // pair + step // pair) % pairs * pair + (my + step) % pair
+        return remote(req_out.at[peer], req_in.at[my], req_send.at[step], req_recv.at[my], replica(peer), me)
+
+    @pl.loop(1, n_peers)
     def _(step):
         req_copy(step).start()
 
-    for k in range(W_FIRST, W_FIRST + W_NEXT):
+    for k in range(w_first, w_first + w_next):
         w_copy(k).start()
 
     for copy in own_sends[2:]:
@@ -206,48 +223,52 @@
     start_c()
     forward()
 
+    def peer_slots(peer):
+        return pl.ds(pl.multiple_of(peer * 2 * CAP, 2 * CAP), 2 * CAP)
+
     def row_copy(peer):
         return remote(
-            picked.at[pl.ds(pl.multiple_of(peer * CAP, CAP), CAP)],
-            fetched.at[pl.ds(pl.multiple_of(rep * CAP, CAP), CAP)],
-            row_send.at[peer], row_recv.at[rep], peer, me,
+            picked.at[peer_slots(peer)], fetched.at[peer_slots(my)],
+            row_send.at[peer], row_recv.at[my], replica(peer), me,
         )
+
+    table_other = table.at[1 - side]
+    remote(table_other, table_other, table_send.at[0], table_recv.at[0], across_z, me).wait_recv()
 
     @pl.loop(0, pairs)
     def _(turn):
-        first = (rep // pair + pairs - turn) % pairs * pair
+        first = (my // pair + pairs - turn) % pairs * pair
         for j in range(pair):
-            sender = first + (rep + j) % pair
-
-            @pl.when(sender != rep)
+            sender = first + (my + j) % pair
+
+            @pl.when(sender != my)
             def _():
                 remote(
-                    req_out.at[sender], req_in.at[sender], req_send.at[0], req_recv.at[sender], sender, me
+                    req_out.at[sender], req_in.at[sender], req_send.at[0], req_recv.at[sender], replica(sender), me
                 ).wait_recv()
 
         columns = []
-        for g in range(2):
-            wanted = req_in[first + g * per_tile]
-            for j in range(1, per_tile):
-                wanted = wanted + req_in[first + g * per_tile + j]
+        for g in range(pair // 2):
+            wanted = req_in[first + 2 * g] + req_in[first + 2 * g + 1]
             columns.append(jnp.broadcast_to(wanted, (8, 128)).T[:, :1])
-        wanted_col = jnp.concatenate(columns, axis=0)
-        hit = lax.broadcasted_iota(jnp.int32, (256, table.shape[0]), 1).astype(F32) + 1.0 == wanted_col
-        picked[pl.ds(pl.multiple_of(first * CAP, 256), 256)] = dot(
-            jnp.where(hit, 1.0, 0.0).astype(BF16), table[...], NN
-        ).astype(BF16)
+        row_iota = lax.broadcasted_iota(jnp.int32, (pair * CAP, table.shape[1]), 1).astype(F32) + 1.0
+        for b in range(2):
+            wanted_col = jnp.concatenate([c[b * 2 * CAP : (b + 1) * 2 * CAP] for c in columns], axis=0)
+            found = dot(jnp.where(row_iota == wanted_col, 1.0, 0.0).astype(BF16), table[b], NN).astype(BF16)
+            for j in range(pair):
+                slots = pl.ds(pl.multiple_of((first + j) * 2 * CAP + b * CAP, CAP), CAP)
+                picked[slots] = found[j * CAP : (j + 1) * CAP]
         for j in range(pair):
-            peer = first + (rep + j) % pair
-
-            @pl.when(peer != rep)
+            peer = first + (my + j) % pair
+
+            @pl.when(peer != my)
             def _():
                 row_copy(peer).start()
 
-    for k in range(W_FIRST + W_NEXT, W_CHUNKS):
+    for k in range(w_first + w_next, W_CHUNKS):
         w_copy(k).start()
 
-    own_slots = pl.ds(pl.multiple_of(rep * CAP, CAP), CAP)
-    fetched[own_slots] = picked[own_slots]
+    fetched[peer_slots(my)] = picked[peer_slots(my)]
 
     tile = 256
     for copy in local:
@@ -273,18 +294,18 @@
     def embed(begin, end):
         @pl.loop(begin, end)
         def _(turn):
-            first = (rep // pair + turn) % pairs * pair
+            first = (my // pair + turn) % pairs * pair
             for j in range(pair):
                 v = first + j
 
-                @pl.when(v != rep)
+                @pl.when(v != my)
                 def _():
-                    slots = pl.ds(pl.multiple_of(v * CAP, CAP), CAP)
                     remote(
-                        picked.at[slots], fetched.at[slots], row_send.at[v], row_recv.at[v], v, me
+                        picked.at[peer_slots(v)], fetched.at[peer_slots(v)],
+                        row_send.at[v], row_recv.at[v], replica(v), me,
                     ).wait_recv()
 
-            slots = pl.ds(pl.multiple_of(first * CAP, pair * CAP), pair * CAP)
+            slots = pl.ds(pl.multiple_of(first * 2 * CAP, pair * 2 * CAP), pair * 2 * CAP)
             rows_t = fetched[slots].T
             stream_t[...] += dot(rows_t, place_of[slots], NN)
 
@@ -312,10 +333,12 @@
             ids_copy(step).wait_send()
             c_copy(step).wait_send()
 
-        @pl.loop(1, n_rep)
+        table_copy.wait_send()
+
+        @pl.loop(1, n_peers)
         def _(step):
             req_copy(step).wait_send()
-            row_copy((rep + step) % n_rep).wait_send()
+            row_copy((my + step) % n_peers).wait_send()
 
         for k in range(W_CHUNKS):
             w_copy(k).wait_send()
@@ -351,8 +374,8 @@
         h_wait(other_across, 1)
         turn_heads(other_across)
 
-    late = pairs - 2
-    early = W_FIRST + W_NEXT
+    late = pairs - 1
+    early = w_first + w_next
     if level == 0:
         for k in range(W_CHUNKS):
             mix(k)
@@ -440,9 +463,9 @@
             pltpu.VMEM((heads_width, all_tokens), BF16),
             pltpu.VMEM((n_fsdp, tokens, width), BF16),
             pltpu.VMEM((width, all_tokens), F32),
-            pltpu.VMEM((vocab_pad, width), BF16),
-            pltpu.VMEM((n_rep, 1, 128), F32),
-            pltpu.VMEM((n_rep, 1, 128), F32),
+            pltpu.VMEM((2, vocab_pad, width), BF16),
+            pltpu.VMEM((n_rep // 2, 1, 128), F32),
+            pltpu.VMEM((n_rep // 2, 1, 128), F32),
             pltpu.VMEM((slots, width), BF16),
             pltpu.VMEM((slots, width), BF16),
             pltpu.VMEM((width, rows), BF16),
@@ -456,10 +479,10 @@
             dma((W_CHUNKS,)), dma((W_CHUNKS,)),
             dma((14,)), dma((n_fsdp, 2)),
             dma((n_fsdp,)), dma((n_fsdp,)),
-            dma((n_rep,)), dma((n_rep,)),
-            dma((n_rep,)), dma((n_rep,)),
+            dma((n_rep // 2,)), dma((n_rep // 2,)),
+            dma((n_rep // 2,)), dma((n_rep // 2,)),
             dma((n_fsdp,)), dma((n_fsdp,)),
-            dma((3,)), dma((rows // 512,)),
+            dma((3,)), dma((rows // 512,)), dma((1,)), dma((1,)),
         ],
         compiler_params=pltpu.CompilerParams(
             collective_id=level, has_side_effects=True, vmem_limit_bytes=44 * 1024 * 1024

time: 106 us -> 98.9 us (0.933)
  the two profiles are of different devices: /device:TPU:57 before, /device:TPU:1 now
where the time goes in v3:
time: 98.9 us; the launch traced here: 98.7 us
  Pallas kernels  96.1 us (97%)
  local copies, waits for them, and re-layouts  1.65 us (2%)
    pallas_call x1, Pallas kernels, local(): lax.switch(mix_step[0] % MIXBITS, branches, token_ids, weights[0], head_o...  96.1 us

profile of v3, /device:TPU:1, one launch (start us, length us, event | category | flops | bytes accessed | tf_op | source)
XLA Modules:
  0.0 98.7 jit_solution(16378143700460817114)
XLA Ops:
  0.7 0.0 copy-start
  0.7 0.0 copy-start.1
  0.7 0.7 copy-done
  1.4 0.0 copy-done.1
  1.4 96.4 %conditional.1 = (bf16[1,2048,256]{2,1,0:T(8,128)(2,1)S(1)}) conditional(s32[]{:T(128)} %clamp.3, (s32[1,128]{1,0:T(1,128)S(1)}, bf16[2048,256]{1,0:T(8,128)(2,1)}, bf16[128,2048]{1,0:T(8,128)(2,1)}, bf16[128,2048]{1,0:T(8,128)(2,1)}, bf16[500,256]{1,0:T(8,128)(2,1)}, /*index=5*/f32[1,2048]{1,0:T(1,128)S(1)}) %tuple.46, ...), branch_computations={%region_0.1_spmd, %region_1.2_spmd, %region_2.3_spmd, %region_3.4_... | conditional | flops 3221225472 | bytes 4194312 | solution.py:501
  1.4 96.1 %step_level_1.1 = bf16[2048,256]{1,0:T(8,128)(2,1)S(1)} custom-call(s32[1,128]{1,0:T(1,128)S(1)} %get-tuple-element.65.ids_ref, bf16[2048,256]{1,0:T(8,128)(2,1)} %get-tuple-element.66.w_ref, bf16[128,2048]{1,0:T(8,128)(2,1)} %get-tuple-element.67.h_ref, bf16[128,2048]{1,0:T(8,128)(2,1)} %get-tuple-element.68.c_ref, ...), custom_call_target="tpu_custom_call" | custom-call | flops 3221225472 | bytes 4194304 | tf_op jit(solution)/shard_map/cond/branch_1_fun/step_level_1/pallas_call | solution.py:501
  97.7 1.0 copy.18
Async XLA Ops:
  0.7 0.7 copy-start
  0.7 0.7 copy-start.1

commit v4 on v3

--- a/solution.py
+++ b/solution.py
@@ -93,8 +93,6 @@
     ids_all[me] = ids_ref[...]
     table[side] = jnp.zeros(table.shape[1:], BF16)
     table[side, :vocab] = tab_ref[...]
-    gain = gain_ref[:, pl.ds(pl.multiple_of(me * width, width), width)]
-    gain_col[...] = jnp.broadcast_to(gain, (128, width)).T
 
     pl.semaphore_wait(barrier, n_fsdp - 1 + n_peers)
 
@@ -146,6 +144,8 @@
             cot.at[me], c_send.at[step], c_recv.at[me], rep, peer,
         )
 
+    gain = gain_ref[:, pl.ds(pl.multiple_of(me * width, width), width)]
+    gain_col[...] = jnp.broadcast_to(gain, (128, width)).T
     earlier = jnp.where(
         lax.broadcasted_iota(jnp.int32, (tokens, tokens), 0) < lax.broadcasted_iota(jnp.int32, (tokens, tokens), 1),
         1.0,
@@ -408,7 +408,7 @@
         peer = (me + step) % n_fsdp
         return remote(stat_out, stat_in.at[me], stat_send.at[step], stat_recv.at[me], rep, peer)
 
-    for step in range(1, n_fsdp):
+    for step in sorted(range(1, n_fsdp), key=lambda step: abs(2 * step - n_fsdp)):
         stat_copy(step).start()
     stat_in[me] = stat_out[...]
     for step in range(1, n_fsdp):

time: 98.9 us -> 103 us (1.041); the launches traced: 98.7 us -> 101 us
  Pallas kernels: 96.1 us -> 98.8 us
    pallas_call x1, Pallas kernels: 96.1 us -> 98.8 us  [local(): lax.switch(mix_step[0] % MIXBITS, branches, token_ids, weights[0], head_o...]
where the time goes in v4:
time: 103 us; the launch traced here: 101 us
  Pallas kernels  98.8 us (96%)
  local copies, waits for them, and re-layouts  1.65 us (2%)
    pallas_call x1, Pallas kernels, local(): lax.switch(mix_step[0] % MIXBITS, branches, token_ids, weights[0], head_o...  98.8 us

profile of v4, /device:TPU:1, one launch (start us, length us, event | category | flops | bytes accessed | tf_op | source)
XLA Modules:
  0.0 101.1 jit_solution(18381677906988614495)
XLA Ops:
  0.7 0.0 copy-start
  0.7 0.0 copy-start.1
  0.7 0.7 copy-done
  1.4 0.0 copy-done.1
  1.4 98.8 %conditional.1 = (bf16[1,2048,256]{2,1,0:T(8,128)(2,1)S(1)}) conditional(s32[]{:T(128)} %clamp.3, (s32[1,128]{1,0:T(1,128)S(1)}, bf16[2048,256]{1,0:T(8,128)(2,1)}, bf16[128,2048]{1,0:T(8,128)(2,1)}, bf16[128,2048]{1,0:T(8,128)(2,1)}, bf16[500,256]{1,0:T(8,128)(2,1)}, /*index=5*/f32[1,2048]{1,0:T(1,128)S(1)}) %tuple.46, ...), branch_computations={%region_0.1_spmd, %region_1.2_spmd, %region_2.3_spmd, %region_3.4_... | conditional | flops 3221225472 | bytes 4194312 | solution.py:501
  1.4 98.8 %step_level_2.1 = bf16[2048,256]{1,0:T(8,128)(2,1)S(1)} custom-call(s32[1,128]{1,0:T(1,128)S(1)} %get-tuple-element.71.ids_ref, bf16[2048,256]{1,0:T(8,128)(2,1)} %get-tuple-element.72.w_ref, bf16[128,2048]{1,0:T(8,128)(2,1)} %get-tuple-element.73.h_ref, bf16[128,2048]{1,0:T(8,128)(2,1)} %get-tuple-element.74.c_ref, ...), custom_call_target="tpu_custom_call" | custom-call | flops 3221225472 | bytes 4194304 | tf_op jit(solution)/shard_map/cond/branch_2_fun/step_level_2/pallas_call | solution.py:501
  100.1 1.0 copy.18
Async XLA Ops:
  0.7 0.7 copy-start
  0.7 0.7 copy-start.1
